TPU v7x, 512 devices: a whole 4x4x16 slice. The times are simulated.
512 devices in a mesh: scen: 4 (over x), gx: 8 (over y, core), gy: 16 (over z).
Axes of the slice: x: 4, y: 4, z: 16, core: 2. Of those that a mesh axis runs over, the one named last changes fastest.
Arguments:
- perm_log: float32 [2, 512, 2048], P(None, 'gx', 'gy'), may hold values from -2.5 to 2.5
- facies: int32 [2, 512, 2048], P(None, 'gx', 'gy'), may hold values from 0 to 3
- facies_scale: float32 [4], replicated, may hold values from 0.5 to 2
- accumulation: float32 [2, 512, 2048], P(None, 'gx', 'gy'), may hold values from 0.05 to 0.5
- previous_pressure: float32 [4, 2, 512, 2048], P('scen', None, 'gx', 'gy'), may hold values from -6 to 6
- observed: float32 [4, 2, 512, 2048], P('scen', None, 'gx', 'gy'), may hold values from -6 to 6
- well_cells: int32 [4, 5], P('scen'), may hold values from 0 to 2097151
- well_rates: float32 [4, 5], P('scen'), may hold values from 5 to 20
Outputs:
- pressure: float32 [4, 2, 512, 2048], P('scen', None, 'gx', 'gy')
- adjoint: float32 [4, 2, 512, 2048], P('scen', None, 'gx', 'gy')
- gradient: float32 [2, 512, 2048], P(None, 'gx', 'gy')
Inputs may be any that keep to these rules, and one draw needn't show every extreme that they name: `well_cells`: a flat index layer * 512 * 2048 + row * 2048 + column of a grid cell; several wells may share a cell.
All inputs are finite; a program needn't handle non-finite values.
Results may differ from a plain program's by a relative error of at most 0.0001.
Values sent between devices are 32-bit elements; how exact they have to be, the bound alone decides.
A program may use at most 128 MiB of HBM per device.

v0:
```python
from functools import partial
import jax
import jax.numpy as jnp
from jax import lax
from jax.sharding import PartitionSpec as P

WELLS = 5
FACIES = 4
SMOOTH = 2
COARSE = 4
vertical = 0.3
damping = 0.8


def extended(block, sides, width):
    for axis, dim in sides:
        count = lax.axis_size(axis)
        forward = [(i, i + 1) for i in range(count - 1)]
        backward = [(target, source) for source, target in forward]
        low = lax.ppermute(
            lax.slice_in_dim(block, block.shape[dim] - width, None, axis=dim), axis, forward
        )
        high = lax.ppermute(lax.slice_in_dim(block, 0, width, axis=dim), axis, backward)
        block = jnp.concatenate([low, block, high], axis=dim)
    return block


def passed_along(value, axis, steps):
    count = lax.axis_size(axis)
    first, last = (max(0, -steps), min(count, count - steps))
    return lax.ppermute(value, axis, [(source, source + steps) for source in range(first, last)])


def partner(value, axis, distance):
    return lax.ppermute(value, axis, [(i, i ^ 1 << distance) for i in range(lax.axis_size(axis))])


def harmonic(left, right):
    return 2.0 * left * right / (left + right)


def planar(padded):
    return (
        padded[..., :-2, 1:-1],
        padded[..., 2:, 1:-1],
        padded[..., 1:-1, :-2],
        padded[..., 1:-1, 2:],
    )


def layer_pair(values):
    padded = jnp.pad(values, ((1, 1), (0, 0), (0, 0)))
    return (padded[:-2], padded[2:])


def build_coeffs(permeability, beside, accumulation):
    below, above = layer_pair(permeability)
    return jnp.stack(
        [
            harmonic(permeability, beside[0]),
            harmonic(permeability, beside[1]),
            harmonic(permeability, beside[2]),
            harmonic(permeability, beside[3]),
            vertical * harmonic(permeability, below),
            vertical * harmonic(permeability, above),
            accumulation,
        ]
    )


def coarsen(coeffs):
    member_count, layer_count, row_count, col_count = coeffs.shape
    quads = coeffs.reshape(member_count, layer_count, row_count // 2, 2, col_count // 2, 2)
    return jnp.stack(
        [
            quads[0, :, :, 0, :, 0] + quads[0, :, :, 0, :, 1],
            quads[1, :, :, 1, :, 0] + quads[1, :, :, 1, :, 1],
            quads[2, :, :, 0, :, 0] + quads[2, :, :, 1, :, 0],
            quads[3, :, :, 0, :, 1] + quads[3, :, :, 1, :, 1],
            jnp.sum(quads[4], (2, 4)),
            jnp.sum(quads[5], (2, 4)),
            jnp.sum(quads[6], (2, 4)),
        ]
    )


def restrict(values):
    layer_count, row_count, col_count = values.shape
    return values.reshape(layer_count, row_count // 2, 2, col_count // 2, 2).sum((2, 4))


def upsample(values):
    return jnp.repeat(jnp.repeat(values, 2, 1), 2, 2)


def parity(bit_number):
    return lax.axis_index("gy") // 2**bit_number % 2


def join_halves(own_half, other_half, bit_number, axis_number):
    lower = parity(bit_number) == 0
    first = jnp.where(lower, own_half, other_half)
    second = jnp.where(lower, other_half, own_half)
    return jnp.concatenate([first, second], axis_number)


def take_half(values, bit_number):
    half_width = values.shape[2] // 2
    return lax.dynamic_slice_in_dim(values, parity(bit_number) * half_width, half_width, 2)


def fine_neighbours(values):
    return planar(extended(values, (("gx", 1), ("gy", 2)), 1))


def coarse_neighbours(values, distance):
    row_lo = passed_along(values[:, -1:, :], "gx", 1)
    row_hi = passed_along(values[:, :1, :], "gx", -1)
    col_lo = passed_along(values[:, :, -1:], "gy", distance)
    col_hi = passed_along(values[:, :, :1], "gy", -distance)
    return (
        jnp.concatenate([row_lo, values[:, :-1, :]], 1),
        jnp.concatenate([values[:, 1:, :], row_hi], 1),
        jnp.concatenate([col_lo, values[:, :, :-1]], 2),
        jnp.concatenate([values[:, :, 1:], col_hi], 2),
    )


def apply_op(values, grid_level, neighbours):
    coeffs, diagonal = grid_level
    row_lo, row_hi, col_lo, col_hi = neighbours(values)
    layer_lo, layer_hi = layer_pair(values)
    return diagonal * values - (
        coeffs[0] * row_lo
        + coeffs[1] * row_hi
        + coeffs[2] * col_lo
        + coeffs[3] * col_hi
        + coeffs[4] * layer_lo
        + coeffs[5] * layer_hi
    )


def smooth(values, target, grid_level, neighbours, sweeps):
    for _ in range(sweeps):
        values = (
            values + damping * (target - apply_op(values, grid_level, neighbours)) / grid_level[1]
        )
    return values


def lift_middle(values):
    return join_halves(values, partner(values, "gy", 0), 0, 2)


def lift_bottom(values):
    return join_halves(values, partner(values, "gy", 1), 1, 2)


def drop_bottom(values):
    return take_half(values, 1)


def drop_middle(values):
    return take_half(values, 0)


def vcycle(target, initial, grids):
    finest, middle, bottom = grids
    middle_near = partial(coarse_neighbours, distance=2)
    bottom_near = partial(coarse_neighbours, distance=4)
    fine_field = smooth(initial, target, finest, fine_neighbours, SMOOTH)
    middle_target = lift_middle(restrict(target - apply_op(fine_field, finest, fine_neighbours)))
    middle_field = smooth(jnp.zeros_like(middle_target), middle_target, middle, middle_near, SMOOTH)
    bottom_target = lift_bottom(
        restrict(middle_target - apply_op(middle_field, middle, middle_near))
    )
    bottom_field = smooth(jnp.zeros_like(bottom_target), bottom_target, bottom, bottom_near, COARSE)
    middle_field = smooth(
        middle_field + upsample(drop_bottom(bottom_field)),
        middle_target,
        middle,
        middle_near,
        SMOOTH,
    )
    fine_field = fine_field + upsample(drop_middle(middle_field))
    return smooth(fine_field, target, finest, fine_neighbours, SMOOTH)


def face_term(permeability, perm_side, pressure, pressure_side, adjoint, adjoint_side, weight):
    total_perm = permeability + perm_side
    return (
        weight
        * permeability
        * 2.0
        * perm_side
        * perm_side
        / (total_perm * total_perm)
        * (adjoint - adjoint_side)
        * (pressure - pressure_side)
    )


def gradient_terms(permeability, perm_six, pressure, pressure_six, adjoint, adjoint_six):
    weights = (1.0, 1.0, 1.0, 1.0, vertical, vertical)
    total = jnp.zeros_like(permeability)
    for number in range(6):
        total = total + face_term(
            permeability,
            perm_six[number],
            pressure,
            pressure_six[number],
            adjoint,
            adjoint_six[number],
            weights[number],
        )
    return total


def with_diagonal(coeffs):
    return (coeffs, jnp.sum(coeffs, 0))


def shards(
    perm_log,
    facies,
    facies_scale,
    accumulation,
    previous_pressure,
    observed,
    well_cells,
    well_rates,
):
    facies_factor = jnp.zeros_like(perm_log)
    for label in range(FACIES):
        facies_factor = facies_factor + jnp.where(
            facies == label, facies_scale[label], jnp.float32(0.0)
        )
    permeability = jnp.exp(perm_log) * facies_factor
    perm_padded = extended(permeability, (("gx", 1), ("gy", 2)), 1)
    perm_beside = planar(perm_padded)
    coeffs = build_coeffs(permeability, perm_beside, accumulation)
    middle = coarsen(coeffs)
    middle = join_halves(middle, partner(middle, "gy", 0), 0, 3)
    bottom = coarsen(middle)
    bottom = join_halves(bottom, partner(bottom, "gy", 1), 1, 3)
    grids = (with_diagonal(coeffs), with_diagonal(middle), with_diagonal(bottom))
    layer_count, row_count, col_count = perm_log.shape
    total_rows = row_count * lax.axis_size("gx")
    total_cols = col_count * lax.axis_size("gy")
    plane_size = total_rows * total_cols
    well_index = well_cells[0]
    well_rate = well_rates[0]
    layer_of = well_index // plane_size
    remainder = well_index % plane_size
    row_of = remainder // total_cols - lax.axis_index("gx") * row_count
    col_of = remainder % total_cols - lax.axis_index("gy") * col_count
    layer_iota = lax.broadcasted_iota(jnp.int32, perm_log.shape, 0)
    row_iota = lax.broadcasted_iota(jnp.int32, perm_log.shape, 1)
    col_iota = lax.broadcasted_iota(jnp.int32, perm_log.shape, 2)
    source = jnp.zeros_like(perm_log)
    for number in range(WELLS):
        placed = (
            (layer_iota == layer_of[number])
            & (row_iota == row_of[number])
            & (col_iota == col_of[number])
        )
        source = source + jnp.where(placed, well_rate[number], jnp.float32(0.0))
    start_pressure = previous_pressure[0]
    pressure = vcycle(accumulation * start_pressure + source, start_pressure, grids)
    adjoint = vcycle(pressure - observed[0], jnp.zeros_like(pressure), grids)
    states = extended(jnp.stack([pressure, adjoint]), (("gx", 2), ("gy", 3)), 1)
    state_beside = planar(states)
    pressure_six = tuple((shifted[0] for shifted in state_beside)) + layer_pair(pressure)
    adjoint_six = tuple((shifted[1] for shifted in state_beside)) + layer_pair(adjoint)
    perm_six = perm_beside + layer_pair(permeability)
    local_terms = gradient_terms(
        permeability, perm_six, pressure, pressure_six, adjoint, adjoint_six
    )
    gradient = lax.psum(-local_terms, "scen")
    return (pressure[None], adjoint[None], gradient)


def solution(mesh):
    return jax.shard_map(
        shards,
        mesh=mesh,
        in_specs=(
            P(None, "gx", "gy"),
            P(None, "gx", "gy"),
            P(),
            P(None, "gx", "gy"),
            P("scen", None, "gx", "gy"),
            P("scen", None, "gx", "gy"),
            P("scen", None),
            P("scen", None),
        ),
        out_specs=(P("scen", None, "gx", "gy"), P("scen", None, "gx", "gy"), P(None, "gx", "gy")),
        check_vma=False,
    )
```

profile of v0, /device:TPU:8, one launch (start us, length us, event | category | flops | bytes accessed | tf_op | source)
XLA Modules:
  0.0 734.4 jit_solution(14104127745226850391)
XLA Ops:
  52.5 6.3 squeeze.134
  64.7 7.0 collective-permute-start.20
  81.4 5.5 stack.54
  103.5 5.5 stack.55
  135.9 5.5 squeeze.132
  154.2 5.5 squeeze.133
  177.8 5.5 reshape.243
  200.6 9.7 %collective-permute-start.32 = (f32[2,16,1]{2,1,0:T(8,128)}, f32[2,16,1]{2,1,0:T(8,128)}, u32[]{:S(2)}, u32[]{:S(2)}) collective-permute-start(f32[2,16,1]{2,1,0:T(8,128)} %broadcast.184), channel_id=1, source_target_pairs={{0,4},{1,5},{2,6},{3,7},{4,8},{5,9},{6,10},{7,11},{8,12},{9,13},{1... | collective-permute-start | bytes 392 | tf_op jit(solution)/shard_map/ppermute | solution.py:31
  230.7 20.3 %fusion.411 = (f32[1,2,16,1,64,1]{0,5,4,3,2,1:T(1,128)S(1)}, f32[1,2,16,1,64,1]{0,5,4,3,2,1:T(1,128)S(1)}, f32[1,2,16,1,64,1]{0,5,4,3,2,1:T(1,128)}, f32[1,2,16,...) fusion(f32[7,2,16,2,64,2]{0,5,4,3,2,1:T(2,128)} %bitcast.228), kind=kLoop, calls=%fused_computation.732 | loop fusion | bytes 131072 | tf_op jit(solution)/shard_map/slice | solution.py:79
  301.9 5.8 collective-permute-start.30
  309.6 9.0 %collective-permute-done.31 = f32[7,2,16,64]{3,2,1,0:T(8,128)S(1)} collective-permute-done((f32[7,2,16,64]{3,2,1,0:T(8,128)S(1)}, f32[7,2,16,64]{3,2,1,0:T(8,128)S(1)}, u32[]{:S(2)}, u32[]{:S(2)}) %collective-permute-start.31) | collective-permute-done | bytes 57376 | tf_op jit(solution)/shard_map/ppermute | solution.py:35
  321.3 7.2 collective-permute-start.36
  338.3 7.1 collective-permute-start.40
  355.2 7.1 collective-permute-start.44
  384.3 6.8 collective-permute-start.52
  410.3 8.0 %collective-permute-done.57 = f32[2,66,1]{2,1,0:T(8,128)S(1)} collective-permute-done((f32[2,66,1]{2,1,0:T(8,128)S(1)}, f32[2,66,1]{2,1,0:T(8,128)S(1)}, u32[]{:S(2)}, u32[]{:S(2)}) %collective-permute-start.57) | collective-permute-done | bytes 560 | tf_op jit(solution)/shard_map/ppermute | solution.py:23
  440.0 5.8 collective-permute-done.61
  486.1 5.8 reshape.250
  537.1 8.1 %collective-permute-start.84 = (f32[2,16,1]{2,1,0:T(8,128)S(1)}, f32[2,16,1]{2,1,0:T(8,128)S(1)}, u32[]{:S(2)}, u32[]{:S(2)}) collective-permute-start(f32[2,16,1]{2,1,0:T(8,128)S(1)} %get-tuple-element.198), channel_id=1, source_target_pairs={{0,4},{1,5},{2,6},{3,7},{4,8},{5,9},{6,10},{7,11},{8,12},{9,13},{1... | collective-permute-start | bytes 392 | tf_op jit(solution)/shard_map/ppermute | solution.py:31
  555.1 7.1 collective-permute-start.88
  572.1 6.9 collective-permute-start.92
  600.8 6.9 collective-permute-start.100
  629.1 6.0 collective-permute-done.105
  674.1 51.4 %all-reduce.41.cloned.1.call-done = f32[2,64,128]{2,1,0:T(8,128)} async-done(((f32[2,64,128]{2,1,0:T(8,128)}), f32[2,64,128]{2,1,0:T(8,128)}) %all-reduce.41.cloned.1.call-update) | async-done | bytes 65552 | tf_op jit(solution)/shard_map/psum | solution.py:279
  (580 shorter events, 496.9 us)
Async XLA Ops:
  7.2 718.4 %all-reduce.41.cloned.1.call-start = ((), (), s32[]{:S(2)}) async-start(), calls=%async_computation | async-start | bytes 131072 | tf_op jit(solution)/shard_map/psum | solution.py:279
  12.1 30.1 %collective-permute-start = (f32[2,1,128]{2,1,0:T(1,128)S(1)}, f32[2,1,128]{2,1,0:T(1,128)S(1)}, u32[]{:S(2)}, u32[]{:S(2)}) collective-permute-start(f32[2,1,128]{2,1,0:T(1,128)S(1)} %get-tuple-element.102), channel_id=1, source_target_pairs={{0,16},{16,32},{32,48},{48,64},{64,80},{80,96},{96,112},{1,17},{17... | collective-permute-start | bytes 3080 | tf_op jit(solution)/shard_map/ppermute | solution.py:20
  14.0 28.2 %collective-permute-start.1 = (f32[2,1,128]{2,1,0:T(1,128)S(1)}, f32[2,1,128]{2,1,0:T(1,128)S(1)}, u32[]{:S(2)}, u32[]{:S(2)}) collective-permute-start(f32[2,1,128]{2,1,0:T(1,128)S(1)} %get-tuple-element.101), channel_id=1, source_target_pairs={{16,0},{32,16},{48,32},{64,48},{80,64},{96,80},{112,96},{17,1},{33... | collective-permute-start | bytes 3080 | tf_op jit(solution)/shard_map/ppermute | solution.py:23
  18.4 27.3 %collective-permute-start.4 = (f32[2,1,128]{2,1,0:T(1,128)S(1)}, f32[2,1,128]{2,1,0:T(1,128)S(1)}, u32[]{:S(2)}, u32[]{:S(2)}) collective-permute-start(f32[2,1,128]{2,1,0:T(1,128)S(1)} %get-tuple-element.103), channel_id=1, source_target_pairs={{0,16},{16,32},{32,48},{48,64},{64,80},{80,96},{96,112},{1,17},{17... | collective-permute-start | bytes 3080 | tf_op jit(solution)/shard_map/ppermute | solution.py:20
  20.3 25.4 %collective-permute-start.5 = (f32[2,1,128]{2,1,0:T(1,128)S(1)}, f32[2,1,128]{2,1,0:T(1,128)S(1)}, u32[]{:S(2)}, u32[]{:S(2)}) collective-permute-start(f32[2,1,128]{2,1,0:T(1,128)S(1)} %get-tuple-element.104), channel_id=1, source_target_pairs={{16,0},{32,16},{48,32},{64,48},{80,64},{96,80},{112,96},{17,1},{33... | collective-permute-start | bytes 3080 | tf_op jit(solution)/shard_map/ppermute | solution.py:23
  26.4 185.1 %collective-permute-start.18 = (f32[2,1,128]{2,1,0:T(1,128)}, f32[2,1,128]{2,1,0:T(1,128)}, u32[]{:S(2)}, u32[]{:S(2)}) collective-permute-start(f32[2,1,128]{2,1,0:T(1,128)} %broadcast.180), channel_id=1, source_target_pairs={{0,16},{16,32},{32,48},{48,64},{64,80},{80,96},{96,112},{1,17},{17... | collective-permute-start | bytes 3080 | tf_op jit(solution)/shard_map/ppermute | solution.py:31
  42.4 19.3 %collective-permute-start.2 = (f32[2,66,1]{2,1,0:T(8,128)S(1)}, f32[2,66,1]{2,1,0:T(8,128)S(1)}, u32[]{:S(2)}, u32[]{:S(2)}) collective-permute-start(f32[2,66,1]{2,1,0:T(8,128)S(1)} %get-tuple-element.78), channel_id=1, source_target_pairs={{0,1},{1,2},{2,3},{3,4},{4,5},{5,6},{6,7},{7,8},{8,9},{9,10},{10,1... | collective-permute-start | bytes 1592 | tf_op jit(solution)/shard_map/ppermute | solution.py:20
  44.4 20.3 %collective-permute-start.3 = (f32[2,66,1]{2,1,0:T(8,128)S(1)}, f32[2,66,1]{2,1,0:T(8,128)S(1)}, u32[]{:S(2)}, u32[]{:S(2)}) collective-permute-start(f32[2,66,1]{2,1,0:T(8,128)S(1)} %get-tuple-element.77), channel_id=1, source_target_pairs={{1,0},{2,1},{3,2},{4,3},{5,4},{6,5},{7,6},{8,7},{9,8},{10,9},{11,1... | collective-permute-start | bytes 1592 | tf_op jit(solution)/shard_map/ppermute | solution.py:23
  46.6 25.1 %collective-permute-start.6 = (f32[2,66,1]{2,1,0:T(8,128)S(1)}, f32[2,66,1]{2,1,0:T(8,128)S(1)}, u32[]{:S(2)}, u32[]{:S(2)}) collective-permute-start(f32[2,66,1]{2,1,0:T(8,128)S(1)} %get-tuple-element.79), channel_id=1, source_target_pairs={{0,1},{1,2},{2,3},{3,4},{4,5},{5,6},{6,7},{7,8},{8,9},{9,10},{10,1... | collective-permute-start | bytes 1592 | tf_op jit(solution)/shard_map/ppermute | solution.py:20
  51.2 20.5 %collective-permute-start.7 = (f32[2,66,1]{2,1,0:T(8,128)S(1)}, f32[2,66,1]{2,1,0:T(8,128)S(1)}, u32[]{:S(2)}, u32[]{:S(2)}) collective-permute-start(f32[2,66,1]{2,1,0:T(8,128)S(1)} %get-tuple-element.80), channel_id=1, source_target_pairs={{1,0},{2,1},{3,2},{4,3},{5,4},{6,5},{7,6},{8,7},{9,8},{10,9},{11,1... | collective-permute-start | bytes 1592 | tf_op jit(solution)/shard_map/ppermute | solution.py:23
  61.7 149.8 %collective-permute-start.19 = (f32[2,1,128]{2,1,0:T(1,128)}, f32[2,1,128]{2,1,0:T(1,128)}, u32[]{:S(2)}, u32[]{:S(2)}) collective-permute-start(f32[2,1,128]{2,1,0:T(1,128)} %broadcast.180), channel_id=1, source_target_pairs={{16,0},{32,16},{48,32},{64,48},{80,64},{96,80},{112,96},{17,1},{33... | collective-permute-start | bytes 3080 | tf_op jit(solution)/shard_map/ppermute | solution.py:31
  64.7 146.7 %collective-permute-start.20 = (f32[2,32,1]{2,1,0:T(8,128)S(1)}, f32[2,32,1]{2,1,0:T(8,128)S(1)}, u32[]{:S(2)}, u32[]{:S(2)}) collective-permute-start(f32[2,32,1]{2,1,0:T(8,128)S(1)} %broadcast.181), channel_id=1, source_target_pairs={{0,2},{1,3},{2,4},{3,5},{4,6},{5,7},{6,8},{7,9},{8,10},{9,11},{10,... | collective-permute-start | bytes 776 | tf_op jit(solution)/shard_map/ppermute | solution.py:31
  75.3 54.1 %collective-permute-start.8 = (f32[2,1,128]{2,1,0:T(1,128)S(1)}, f32[2,1,128]{2,1,0:T(1,128)S(1)}, u32[]{:S(2)}, u32[]{:S(2)}) collective-permute-start(f32[2,1,128]{2,1,0:T(1,128)S(1)} %get-tuple-element.99), channel_id=1, source_target_pairs={{0,16},{16,32},{32,48},{48,64},{64,80},{80,96},{96,112},{1,17},{17... | collective-permute-start | bytes 3080 | tf_op jit(solution)/shard_map/ppermute | solution.py:20
  77.2 52.2 %collective-permute-start.9 = (f32[2,1,128]{2,1,0:T(1,128)S(1)}, f32[2,1,128]{2,1,0:T(1,128)S(1)}, u32[]{:S(2)}, u32[]{:S(2)}) collective-permute-start(f32[2,1,128]{2,1,0:T(1,128)S(1)} %get-tuple-element.100), channel_id=1, source_target_pairs={{16,0},{32,16},{48,32},{64,48},{80,64},{96,80},{112,96},{17,1},{33... | collective-permute-start | bytes 3080 | tf_op jit(solution)/shard_map/ppermute | solution.py:23
  129.5 14.8 %collective-permute-start.10 = (f32[2,66,1]{2,1,0:T(8,128)S(1)}, f32[2,66,1]{2,1,0:T(8,128)S(1)}, u32[]{:S(2)}, u32[]{:S(2)}) collective-permute-start(f32[2,66,1]{2,1,0:T(8,128)S(1)} %get-tuple-element.73), channel_id=1, source_target_pairs={{0,1},{1,2},{2,3},{3,4},{4,5},{5,6},{6,7},{7,8},{8,9},{9,10},{10,1... | collective-permute-start | bytes 1592 | tf_op jit(solution)/shard_map/ppermute | solution.py:20
  170.1 41.3 %collective-permute-start.21 = (f32[2,32,1]{2,1,0:T(8,128)S(1)}, f32[2,32,1]{2,1,0:T(8,128)S(1)}, u32[]{:S(2)}, u32[]{:S(2)}) collective-permute-start(f32[2,32,1]{2,1,0:T(8,128)S(1)} %broadcast.181), channel_id=1, source_target_pairs={{2,0},{3,1},{4,2},{5,3},{6,4},{7,5},{8,6},{9,7},{10,8},{11,9},{12,... | collective-permute-start | bytes 776 | tf_op jit(solution)/shard_map/ppermute | solution.py:31
  200.6 119.1 %collective-permute-start.32 = (f32[2,16,1]{2,1,0:T(8,128)}, f32[2,16,1]{2,1,0:T(8,128)}, u32[]{:S(2)}, u32[]{:S(2)}) collective-permute-start(f32[2,16,1]{2,1,0:T(8,128)} %broadcast.184), channel_id=1, source_target_pairs={{0,4},{1,5},{2,6},{3,7},{4,8},{5,9},{6,10},{7,11},{8,12},{9,13},{1... | collective-permute-start | bytes 392 | tf_op jit(solution)/shard_map/ppermute | solution.py:31
  216.2 68.4 %collective-permute-start.24 = (f32[2,32,1]{2,1,0:T(8,128)}, f32[2,32,1]{2,1,0:T(8,128)}, u32[]{:S(2)}, u32[]{:S(2)}) collective-permute-start(f32[2,32,1]{2,1,0:T(8,128)} %get-tuple-element.172), channel_id=1, source_target_pairs={{0,2},{1,3},{2,4},{3,5},{4,6},{5,7},{6,8},{7,9},{8,10},{9,11},{10,... | collective-permute-start | bytes 776 | tf_op jit(solution)/shard_map/ppermute | solution.py:31
  220.9 63.6 %collective-permute-start.25 = (f32[2,32,1]{2,1,0:T(8,128)}, f32[2,32,1]{2,1,0:T(8,128)}, u32[]{:S(2)}, u32[]{:S(2)}) collective-permute-start(f32[2,32,1]{2,1,0:T(8,128)} %get-tuple-element.171), channel_id=1, source_target_pairs={{2,0},{3,1},{4,2},{5,3},{6,4},{7,5},{8,6},{9,7},{10,8},{11,9},{12,... | collective-permute-start | bytes 776 | tf_op jit(solution)/shard_map/ppermute | solution.py:31
  222.2 62.3 %collective-permute-start.22 = (f32[2,1,128]{2,1,0:T(1,128)}, f32[2,1,128]{2,1,0:T(1,128)}, u32[]{:S(2)}, u32[]{:S(2)}) collective-permute-start(f32[2,1,128]{2,1,0:T(1,128)} %get-tuple-element.176), channel_id=1, source_target_pairs={{0,16},{16,32},{32,48},{48,64},{64,80},{80,96},{96,112},{1,17},{17... | collective-permute-start | bytes 3080 | tf_op jit(solution)/shard_map/ppermute | solution.py:31
  224.2 60.4 %collective-permute-start.23 = (f32[2,1,128]{2,1,0:T(1,128)}, f32[2,1,128]{2,1,0:T(1,128)}, u32[]{:S(2)}, u32[]{:S(2)}) collective-permute-start(f32[2,1,128]{2,1,0:T(1,128)} %get-tuple-element.175), channel_id=1, source_target_pairs={{16,0},{32,16},{48,32},{64,48},{80,64},{96,80},{112,96},{17,1},{33... | collective-permute-start | bytes 3080 | tf_op jit(solution)/shard_map/ppermute | solution.py:31
  298.0 21.7 %collective-permute-start.33 = (f32[2,16,1]{2,1,0:T(8,128)}, f32[2,16,1]{2,1,0:T(8,128)S(1)}, u32[]{:S(2)}, u32[]{:S(2)}) collective-permute-start(f32[2,16,1]{2,1,0:T(8,128)} %broadcast.184), channel_id=1, source_target_pairs={{4,0},{5,1},{6,2},{7,3},{8,4},{9,5},{10,6},{11,7},{12,8},{13,9},{1... | collective-permute-start | bytes 392 | tf_op jit(solution)/shard_map/ppermute | solution.py:31
  321.3 14.1 %collective-permute-start.36 = (f32[2,16,1]{2,1,0:T(8,128)S(1)}, f32[2,16,1]{2,1,0:T(8,128)S(1)}, u32[]{:S(2)}, u32[]{:S(2)}) collective-permute-start(f32[2,16,1]{2,1,0:T(8,128)S(1)} %get-tuple-element.224), channel_id=1, source_target_pairs={{0,4},{1,5},{2,6},{3,7},{4,8},{5,9},{6,10},{7,11},{8,12},{9,13},{1... | collective-permute-start | bytes 392 | tf_op jit(solution)/shard_map/ppermute | solution.py:31
  537.1 15.0 %collective-permute-start.84 = (f32[2,16,1]{2,1,0:T(8,128)S(1)}, f32[2,16,1]{2,1,0:T(8,128)S(1)}, u32[]{:S(2)}, u32[]{:S(2)}) collective-permute-start(f32[2,16,1]{2,1,0:T(8,128)S(1)} %get-tuple-element.198), channel_id=1, source_target_pairs={{0,4},{1,5},{2,6},{3,7},{4,8},{5,9},{6,10},{7,11},{8,12},{9,13},{1... | collective-permute-start | bytes 392 | tf_op jit(solution)/shard_map/ppermute | solution.py:31
  (160 other events, 3573.6 us)
Sparse Core Ops, SparseCore 0:
  674.3 51.2 all-reduce.40
where the time goes:
time: 743 us; the launch traced here: 734 us
  starting transfers between devices  353 us (48%)
  waiting for transfers between devices  153 us (21%)
  local copies, waits for them, and re-layouts  146 us (20%)
  other arithmetic  65.3 us (9%)
  between operations  17.6 us (2%)
    ppermute x62, starting transfers between devices, passed_along(): lax.ppermute(value, axis, [(source, source + steps) for source in range(f...  201 us
    ppermute x23, starting transfers between devices, extended(): lax.ppermute(lax.slice_in_dim(block, block.shape[dim] - width, None, axis...  72.1 us
    ppermute x23, starting transfers between devices, extended(): lax.ppermute(lax.slice_in_dim(block, 0, width, axis=dim), axis, backward)  55.3 us
    psum x1, waiting for transfers between devices, shards(): gradient = lax.psum(-local_terms, 'scen')  51.4 us
    ppermute x23, waiting for transfers between devices, extended(): lax.ppermute(lax.slice_in_dim(block, 0, width, axis=dim), axis, backward)  48.7 us
    unnamed x158, local copies, waits for them, and re-layouts  34.5 us
    ppermute x62, waiting for transfers between devices, passed_along(): lax.ppermute(value, axis, [(source, source + steps) for source in range(f...  26.7 us
    slice x2, local copies, waits for them, and re-layouts, coarsen(): quads[3, :, :, 1, :, 1]  25 us
  transfers between devices with their start and end apart: 115, of which 41 were waited for; matrix products, arithmetic and copies ran while one was open for 24% of the time, Pallas kernels for 0%

commit v1 on v0

--- a/solution.py
+++ b/solution.py
@@ -276,7 +276,7 @@
     local_terms = gradient_terms(
         permeability, perm_six, pressure, pressure_six, adjoint, adjoint_six
     )
-    gradient = lax.psum(-local_terms, "scen")
+    gradient = jnp.sum(lax.all_gather(-local_terms, "scen"), axis=0)
     return (pressure[None], adjoint[None], gradient)
 
 

time: 743 us -> 689 us (0.927)
  the two profiles are of different devices: /device:TPU:8 before, /device:TPU:10 now
where the time goes in v1:
time: 689 us; the launch traced here: 681 us
  starting transfers between devices  353 us (51%)
  local copies, waits for them, and re-layouts  144 us (21%)
  waiting for transfers between devices  101 us (15%)
  other arithmetic  65.5 us (10%)
  blocking collectives  12.6 us (2%)
    ppermute x62, starting transfers between devices, passed_along(): lax.ppermute(value, axis, [(source, source + steps) for source in range(f...  201 us
    ppermute x23, starting transfers between devices, extended(): lax.ppermute(lax.slice_in_dim(block, block.shape[dim] - width, None, axis...  73.9 us
    ppermute x23, starting transfers between devices, extended(): lax.ppermute(lax.slice_in_dim(block, 0, width, axis=dim), axis, backward)  53.5 us
    ppermute x23, waiting for transfers between devices, extended(): lax.ppermute(lax.slice_in_dim(block, 0, width, axis=dim), axis, backward)  48.7 us
    unnamed x157, local copies, waits for them, and re-layouts  33 us
    ppermute x62, waiting for transfers between devices, passed_along(): lax.ppermute(value, axis, [(source, source + steps) for source in range(f...  26.7 us
    slice x2, local copies, waits for them, and re-layouts, coarsen(): quads[3, :, :, 1, :, 1]  24.9 us
    ppermute x6, starting transfers between devices, partner(): lax.ppermute(value, axis, [(i, i ^ 1 << distance) for i in range(lax.axis...  24.8 us
  transfers between devices with their start and end apart: 114, of which 40 were waited for; matrix products, arithmetic and copies ran while one was open for 26% of the time, Pallas kernels for 0%

profile of v1, /device:TPU:10, one launch (start us, length us, event | category | flops | bytes accessed | tf_op | source)
XLA Modules:
  0.0 680.6 jit_solution(6424257479658595382)
XLA Ops:
  46.1 6.3 squeeze.134
  58.2 7.0 %collective-permute-start.20 = (f32[2,32,1]{2,1,0:T(8,128)S(1)}, f32[2,32,1]{2,1,0:T(8,128)S(1)}, u32[]{:S(2)}, u32[]{:S(2)}) collective-permute-start(f32[2,32,1]{2,1,0:T(8,128)S(1)} %broadcast.181), channel_id=1, source_target_pairs={{0,2},{1,3},{2,4},{3,5},{4,6},{5,7},{6,8},{7,9},{8,10},{9,11},{10,... | collective-permute-start | bytes 776 | tf_op jit(solution)/shard_map/ppermute | solution.py:31
  75.0 5.5 stack.54
  97.0 5.5 stack.55
  129.3 5.5 squeeze.132
  147.6 5.5 squeeze.133
  171.3 5.5 reshape.243
  194.2 9.7 %collective-permute-start.32 = (f32[2,16,1]{2,1,0:T(8,128)}, f32[2,16,1]{2,1,0:T(8,128)}, u32[]{:S(2)}, u32[]{:S(2)}) collective-permute-start(f32[2,16,1]{2,1,0:T(8,128)} %broadcast.184), channel_id=1, source_target_pairs={{0,4},{1,5},{2,6},{3,7},{4,8},{5,9},{6,10},{7,11},{8,12},{9,13},{1... | collective-permute-start | bytes 392 | tf_op jit(solution)/shard_map/ppermute | solution.py:31
  224.2 20.2 %fusion.411 = (f32[1,2,16,1,64,1]{0,5,4,3,2,1:T(1,128)S(1)}, f32[1,2,16,1,64,1]{0,5,4,3,2,1:T(1,128)S(1)}, f32[1,2,16,1,64,1]{0,5,4,3,2,1:T(1,128)}, f32[1,2,16,...) fusion(f32[7,2,16,2,64,2]{0,5,4,3,2,1:T(2,128)} %bitcast.229), kind=kLoop, calls=%fused_computation.732 | loop fusion | bytes 131072 | tf_op jit(solution)/shard_map/slice | solution.py:79
  295.3 5.8 collective-permute-start.30
  303.0 9.0 %collective-permute-done.31 = f32[7,2,16,64]{3,2,1,0:T(8,128)S(1)} collective-permute-done((f32[7,2,16,64]{3,2,1,0:T(8,128)S(1)}, f32[7,2,16,64]{3,2,1,0:T(8,128)S(1)}, u32[]{:S(2)}, u32[]{:S(2)}) %collective-permute-start.31) | collective-permute-done | bytes 57376 | tf_op jit(solution)/shard_map/ppermute | solution.py:35
  314.7 7.1 %collective-permute-start.36 = (f32[2,16,1]{2,1,0:T(8,128)S(1)}, f32[2,16,1]{2,1,0:T(8,128)S(1)}, u32[]{:S(2)}, u32[]{:S(2)}) collective-permute-start(f32[2,16,1]{2,1,0:T(8,128)S(1)} %get-tuple-element.224), channel_id=1, source_target_pairs={{0,4},{1,5},{2,6},{3,7},{4,8},{5,9},{6,10},{7,11},{8,12},{9,13},{1... | collective-permute-start | bytes 392 | tf_op jit(solution)/shard_map/ppermute | solution.py:31
  331.6 7.1 %collective-permute-start.40 = (f32[2,16,1]{2,1,0:T(8,128)S(1)}, f32[2,16,1]{2,1,0:T(8,128)S(1)}, u32[]{:S(2)}, u32[]{:S(2)}) collective-permute-start(f32[2,16,1]{2,1,0:T(8,128)S(1)} %get-tuple-element.216), channel_id=1, source_target_pairs={{0,4},{1,5},{2,6},{3,7},{4,8},{5,9},{6,10},{7,11},{8,12},{9,13},{1... | collective-permute-start | bytes 392 | tf_op jit(solution)/shard_map/ppermute | solution.py:31
  348.5 7.1 %collective-permute-start.44 = (f32[2,16,1]{2,1,0:T(8,128)S(1)}, f32[2,16,1]{2,1,0:T(8,128)S(1)}, u32[]{:S(2)}, u32[]{:S(2)}) collective-permute-start(f32[2,16,1]{2,1,0:T(8,128)S(1)} %get-tuple-element.208), channel_id=1, source_target_pairs={{0,4},{1,5},{2,6},{3,7},{4,8},{5,9},{6,10},{7,11},{8,12},{9,13},{1... | collective-permute-start | bytes 392 | tf_op jit(solution)/shard_map/ppermute | solution.py:31
  377.6 6.8 %collective-permute-start.52 = (f32[2,32,1]{2,1,0:T(8,128)S(1)}, f32[2,32,1]{2,1,0:T(8,128)S(1)}, u32[]{:S(2)}, u32[]{:S(2)}) collective-permute-start(f32[2,32,1]{2,1,0:T(8,128)S(1)} %get-tuple-element.146), channel_id=1, source_target_pairs={{0,2},{1,3},{2,4},{3,5},{4,6},{5,7},{6,8},{7,9},{8,10},{9,11},{10,... | collective-permute-start | bytes 776 | tf_op jit(solution)/shard_map/ppermute | solution.py:31
  403.6 8.0 %collective-permute-done.57 = f32[2,66,1]{2,1,0:T(8,128)S(1)} collective-permute-done((f32[2,66,1]{2,1,0:T(8,128)S(1)}, f32[2,66,1]{2,1,0:T(8,128)S(1)}, u32[]{:S(2)}, u32[]{:S(2)}) %collective-permute-start.57) | collective-permute-done | bytes 560 | tf_op jit(solution)/shard_map/ppermute | solution.py:23
  433.4 5.8 collective-permute-done.61
  479.5 5.8 reshape.250
  530.5 8.1 %collective-permute-start.84 = (f32[2,16,1]{2,1,0:T(8,128)S(1)}, f32[2,16,1]{2,1,0:T(8,128)S(1)}, u32[]{:S(2)}, u32[]{:S(2)}) collective-permute-start(f32[2,16,1]{2,1,0:T(8,128)S(1)} %get-tuple-element.198), channel_id=1, source_target_pairs={{0,4},{1,5},{2,6},{3,7},{4,8},{5,9},{6,10},{7,11},{8,12},{9,13},{1... | collective-permute-start | bytes 392 | tf_op jit(solution)/shard_map/ppermute | solution.py:31
  548.4 7.1 %collective-permute-start.88 = (f32[2,16,1]{2,1,0:T(8,128)S(1)}, f32[2,16,1]{2,1,0:T(8,128)S(1)}, u32[]{:S(2)}, u32[]{:S(2)}) collective-permute-start(f32[2,16,1]{2,1,0:T(8,128)S(1)} %get-tuple-element.190), channel_id=1, source_target_pairs={{0,4},{1,5},{2,6},{3,7},{4,8},{5,9},{6,10},{7,11},{8,12},{9,13},{1... | collective-permute-start | bytes 392 | tf_op jit(solution)/shard_map/ppermute | solution.py:31
  565.4 6.9 %collective-permute-start.92 = (f32[2,16,1]{2,1,0:T(8,128)S(1)}, f32[2,16,1]{2,1,0:T(8,128)S(1)}, u32[]{:S(2)}, u32[]{:S(2)}) collective-permute-start(f32[2,16,1]{2,1,0:T(8,128)S(1)} %get-tuple-element.182), channel_id=1, source_target_pairs={{0,4},{1,5},{2,6},{3,7},{4,8},{5,9},{6,10},{7,11},{8,12},{9,13},{1... | collective-permute-start | bytes 392 | tf_op jit(solution)/shard_map/ppermute | solution.py:31
  594.2 6.9 %collective-permute-start.100 = (f32[2,32,1]{2,1,0:T(8,128)S(1)}, f32[2,32,1]{2,1,0:T(8,128)S(1)}, u32[]{:S(2)}, u32[]{:S(2)}) collective-permute-start(f32[2,32,1]{2,1,0:T(8,128)S(1)} %get-tuple-element.110), channel_id=1, source_target_pairs={{0,2},{1,3},{2,4},{3,5},{4,6},{5,7},{6,8},{7,9},{8,10},{9,11},{10,... | collective-permute-start | bytes 776 | tf_op jit(solution)/shard_map/ppermute | solution.py:31
  622.5 6.0 collective-permute-done.105
  666.8 12.6 %all-gather = f32[8,64,128]{2,1,0:T(8,128)S(1)} all-gather(f32[2,64,128]{2,1,0:T(8,128)S(1)} %fusion.17), channel_id=2, replica_groups=mesh['scen'=4,'gx'=8,'gy'=16] {'scen'}, dimensions={0}, use_global_device_ids=true | all-gather | bytes 327680 | tf_op jit(solution)/shard_map/all_gather | solution.py:279
  (578 shorter events, 495.4 us)
Async XLA Ops:
  5.5 28.4 %collective-permute-start = (f32[2,1,128]{2,1,0:T(1,128)S(1)}, f32[2,1,128]{2,1,0:T(1,128)S(1)}, u32[]{:S(2)}, u32[]{:S(2)}) collective-permute-start(f32[2,1,128]{2,1,0:T(1,128)S(1)} %get-tuple-element.102), channel_id=1, source_target_pairs={{0,16},{16,32},{32,48},{48,64},{64,80},{80,96},{96,112},{1,17},{17... | collective-permute-start | bytes 3080 | tf_op jit(solution)/shard_map/ppermute | solution.py:20
  7.5 26.5 %collective-permute-start.1 = (f32[2,1,128]{2,1,0:T(1,128)S(1)}, f32[2,1,128]{2,1,0:T(1,128)S(1)}, u32[]{:S(2)}, u32[]{:S(2)}) collective-permute-start(f32[2,1,128]{2,1,0:T(1,128)S(1)} %get-tuple-element.101), channel_id=1, source_target_pairs={{16,0},{32,16},{48,32},{64,48},{80,64},{96,80},{112,96},{17,1},{33... | collective-permute-start | bytes 3080 | tf_op jit(solution)/shard_map/ppermute | solution.py:23
  11.8 27.4 %collective-permute-start.4 = (f32[2,1,128]{2,1,0:T(1,128)S(1)}, f32[2,1,128]{2,1,0:T(1,128)S(1)}, u32[]{:S(2)}, u32[]{:S(2)}) collective-permute-start(f32[2,1,128]{2,1,0:T(1,128)S(1)} %get-tuple-element.103), channel_id=1, source_target_pairs={{0,16},{16,32},{32,48},{48,64},{64,80},{80,96},{96,112},{1,17},{17... | collective-permute-start | bytes 3080 | tf_op jit(solution)/shard_map/ppermute | solution.py:20
  13.8 25.5 %collective-permute-start.5 = (f32[2,1,128]{2,1,0:T(1,128)S(1)}, f32[2,1,128]{2,1,0:T(1,128)S(1)}, u32[]{:S(2)}, u32[]{:S(2)}) collective-permute-start(f32[2,1,128]{2,1,0:T(1,128)S(1)} %get-tuple-element.104), channel_id=1, source_target_pairs={{16,0},{32,16},{48,32},{64,48},{80,64},{96,80},{112,96},{17,1},{33... | collective-permute-start | bytes 3080 | tf_op jit(solution)/shard_map/ppermute | solution.py:23
  18.0 187.0 %collective-permute-start.18 = (f32[2,1,128]{2,1,0:T(1,128)}, f32[2,1,128]{2,1,0:T(1,128)}, u32[]{:S(2)}, u32[]{:S(2)}) collective-permute-start(f32[2,1,128]{2,1,0:T(1,128)} %broadcast.180), channel_id=1, source_target_pairs={{0,16},{16,32},{32,48},{48,64},{64,80},{80,96},{96,112},{1,17},{17... | collective-permute-start | bytes 3080 | tf_op jit(solution)/shard_map/ppermute | solution.py:31
  34.1 21.1 %collective-permute-start.2 = (f32[2,66,1]{2,1,0:T(8,128)S(1)}, f32[2,66,1]{2,1,0:T(8,128)S(1)}, u32[]{:S(2)}, u32[]{:S(2)}) collective-permute-start(f32[2,66,1]{2,1,0:T(8,128)S(1)} %get-tuple-element.78), channel_id=1, source_target_pairs={{0,1},{1,2},{2,3},{3,4},{4,5},{5,6},{6,7},{7,8},{8,9},{9,10},{10,1... | collective-permute-start | bytes 1592 | tf_op jit(solution)/shard_map/ppermute | solution.py:20
  37.9 20.3 %collective-permute-start.3 = (f32[2,66,1]{2,1,0:T(8,128)S(1)}, f32[2,66,1]{2,1,0:T(8,128)S(1)}, u32[]{:S(2)}, u32[]{:S(2)}) collective-permute-start(f32[2,66,1]{2,1,0:T(8,128)S(1)} %get-tuple-element.77), channel_id=1, source_target_pairs={{1,0},{2,1},{3,2},{4,3},{5,4},{6,5},{7,6},{8,7},{9,8},{10,9},{11,1... | collective-permute-start | bytes 1592 | tf_op jit(solution)/shard_map/ppermute | solution.py:23
  40.2 25.1 %collective-permute-start.6 = (f32[2,66,1]{2,1,0:T(8,128)S(1)}, f32[2,66,1]{2,1,0:T(8,128)S(1)}, u32[]{:S(2)}, u32[]{:S(2)}) collective-permute-start(f32[2,66,1]{2,1,0:T(8,128)S(1)} %get-tuple-element.79), channel_id=1, source_target_pairs={{0,1},{1,2},{2,3},{3,4},{4,5},{5,6},{6,7},{7,8},{8,9},{9,10},{10,1... | collective-permute-start | bytes 1592 | tf_op jit(solution)/shard_map/ppermute | solution.py:20
  44.8 20.5 %collective-permute-start.7 = (f32[2,66,1]{2,1,0:T(8,128)S(1)}, f32[2,66,1]{2,1,0:T(8,128)S(1)}, u32[]{:S(2)}, u32[]{:S(2)}) collective-permute-start(f32[2,66,1]{2,1,0:T(8,128)S(1)} %get-tuple-element.80), channel_id=1, source_target_pairs={{1,0},{2,1},{3,2},{4,3},{5,4},{6,5},{7,6},{8,7},{9,8},{10,9},{11,1... | collective-permute-start | bytes 1592 | tf_op jit(solution)/shard_map/ppermute | solution.py:23
  55.2 149.8 %collective-permute-start.19 = (f32[2,1,128]{2,1,0:T(1,128)}, f32[2,1,128]{2,1,0:T(1,128)}, u32[]{:S(2)}, u32[]{:S(2)}) collective-permute-start(f32[2,1,128]{2,1,0:T(1,128)} %broadcast.180), channel_id=1, source_target_pairs={{16,0},{32,16},{48,32},{64,48},{80,64},{96,80},{112,96},{17,1},{33... | collective-permute-start | bytes 3080 | tf_op jit(solution)/shard_map/ppermute | solution.py:31
  58.2 146.7 %collective-permute-start.20 = (f32[2,32,1]{2,1,0:T(8,128)S(1)}, f32[2,32,1]{2,1,0:T(8,128)S(1)}, u32[]{:S(2)}, u32[]{:S(2)}) collective-permute-start(f32[2,32,1]{2,1,0:T(8,128)S(1)} %broadcast.181), channel_id=1, source_target_pairs={{0,2},{1,3},{2,4},{3,5},{4,6},{5,7},{6,8},{7,9},{8,10},{9,11},{10,... | collective-permute-start | bytes 776 | tf_op jit(solution)/shard_map/ppermute | solution.py:31
  68.9 53.9 %collective-permute-start.8 = (f32[2,1,128]{2,1,0:T(1,128)S(1)}, f32[2,1,128]{2,1,0:T(1,128)S(1)}, u32[]{:S(2)}, u32[]{:S(2)}) collective-permute-start(f32[2,1,128]{2,1,0:T(1,128)S(1)} %get-tuple-element.99), channel_id=1, source_target_pairs={{0,16},{16,32},{32,48},{48,64},{64,80},{80,96},{96,112},{1,17},{17... | collective-permute-start | bytes 3080 | tf_op jit(solution)/shard_map/ppermute | solution.py:20
  70.8 52.0 %collective-permute-start.9 = (f32[2,1,128]{2,1,0:T(1,128)S(1)}, f32[2,1,128]{2,1,0:T(1,128)S(1)}, u32[]{:S(2)}, u32[]{:S(2)}) collective-permute-start(f32[2,1,128]{2,1,0:T(1,128)S(1)} %get-tuple-element.100), channel_id=1, source_target_pairs={{16,0},{32,16},{48,32},{64,48},{80,64},{96,80},{112,96},{17,1},{33... | collective-permute-start | bytes 3080 | tf_op jit(solution)/shard_map/ppermute | solution.py:23
  123.0 14.8 %collective-permute-start.10 = (f32[2,66,1]{2,1,0:T(8,128)S(1)}, f32[2,66,1]{2,1,0:T(8,128)S(1)}, u32[]{:S(2)}, u32[]{:S(2)}) collective-permute-start(f32[2,66,1]{2,1,0:T(8,128)S(1)} %get-tuple-element.73), channel_id=1, source_target_pairs={{0,1},{1,2},{2,3},{3,4},{4,5},{5,6},{6,7},{7,8},{8,9},{9,10},{10,1... | collective-permute-start | bytes 1592 | tf_op jit(solution)/shard_map/ppermute | solution.py:20
  163.6 41.4 %collective-permute-start.21 = (f32[2,32,1]{2,1,0:T(8,128)S(1)}, f32[2,32,1]{2,1,0:T(8,128)S(1)}, u32[]{:S(2)}, u32[]{:S(2)}) collective-permute-start(f32[2,32,1]{2,1,0:T(8,128)S(1)} %broadcast.181), channel_id=1, source_target_pairs={{2,0},{3,1},{4,2},{5,3},{6,4},{7,5},{8,6},{9,7},{10,8},{11,9},{12,... | collective-permute-start | bytes 776 | tf_op jit(solution)/shard_map/ppermute | solution.py:31
  194.2 118.9 %collective-permute-start.32 = (f32[2,16,1]{2,1,0:T(8,128)}, f32[2,16,1]{2,1,0:T(8,128)}, u32[]{:S(2)}, u32[]{:S(2)}) collective-permute-start(f32[2,16,1]{2,1,0:T(8,128)} %broadcast.184), channel_id=1, source_target_pairs={{0,4},{1,5},{2,6},{3,7},{4,8},{5,9},{6,10},{7,11},{8,12},{9,13},{1... | collective-permute-start | bytes 392 | tf_op jit(solution)/shard_map/ppermute | solution.py:31
  209.7 68.2 %collective-permute-start.24 = (f32[2,32,1]{2,1,0:T(8,128)}, f32[2,32,1]{2,1,0:T(8,128)}, u32[]{:S(2)}, u32[]{:S(2)}) collective-permute-start(f32[2,32,1]{2,1,0:T(8,128)} %get-tuple-element.172), channel_id=1, source_target_pairs={{0,2},{1,3},{2,4},{3,5},{4,6},{5,7},{6,8},{7,9},{8,10},{9,11},{10,... | collective-permute-start | bytes 776 | tf_op jit(solution)/shard_map/ppermute | solution.py:31
  214.4 63.5 %collective-permute-start.25 = (f32[2,32,1]{2,1,0:T(8,128)}, f32[2,32,1]{2,1,0:T(8,128)}, u32[]{:S(2)}, u32[]{:S(2)}) collective-permute-start(f32[2,32,1]{2,1,0:T(8,128)} %get-tuple-element.171), channel_id=1, source_target_pairs={{2,0},{3,1},{4,2},{5,3},{6,4},{7,5},{8,6},{9,7},{10,8},{11,9},{12,... | collective-permute-start | bytes 776 | tf_op jit(solution)/shard_map/ppermute | solution.py:31
  215.7 62.2 %collective-permute-start.22 = (f32[2,1,128]{2,1,0:T(1,128)}, f32[2,1,128]{2,1,0:T(1,128)}, u32[]{:S(2)}, u32[]{:S(2)}) collective-permute-start(f32[2,1,128]{2,1,0:T(1,128)} %get-tuple-element.176), channel_id=1, source_target_pairs={{0,16},{16,32},{32,48},{48,64},{64,80},{80,96},{96,112},{1,17},{17... | collective-permute-start | bytes 3080 | tf_op jit(solution)/shard_map/ppermute | solution.py:31
  217.6 60.3 %collective-permute-start.23 = (f32[2,1,128]{2,1,0:T(1,128)}, f32[2,1,128]{2,1,0:T(1,128)}, u32[]{:S(2)}, u32[]{:S(2)}) collective-permute-start(f32[2,1,128]{2,1,0:T(1,128)} %get-tuple-element.175), channel_id=1, source_target_pairs={{16,0},{32,16},{48,32},{64,48},{80,64},{96,80},{112,96},{17,1},{33... | collective-permute-start | bytes 3080 | tf_op jit(solution)/shard_map/ppermute | solution.py:31
  291.4 21.7 %collective-permute-start.33 = (f32[2,16,1]{2,1,0:T(8,128)}, f32[2,16,1]{2,1,0:T(8,128)S(1)}, u32[]{:S(2)}, u32[]{:S(2)}) collective-permute-start(f32[2,16,1]{2,1,0:T(8,128)} %broadcast.184), channel_id=1, source_target_pairs={{4,0},{5,1},{6,2},{7,3},{8,4},{9,5},{10,6},{11,7},{12,8},{13,9},{1... | collective-permute-start | bytes 392 | tf_op jit(solution)/shard_map/ppermute | solution.py:31
  314.7 14.0 %collective-permute-start.36 = (f32[2,16,1]{2,1,0:T(8,128)S(1)}, f32[2,16,1]{2,1,0:T(8,128)S(1)}, u32[]{:S(2)}, u32[]{:S(2)}) collective-permute-start(f32[2,16,1]{2,1,0:T(8,128)S(1)} %get-tuple-element.224), channel_id=1, source_target_pairs={{0,4},{1,5},{2,6},{3,7},{4,8},{5,9},{6,10},{7,11},{8,12},{9,13},{1... | collective-permute-start | bytes 392 | tf_op jit(solution)/shard_map/ppermute | solution.py:31
  331.6 14.0 %collective-permute-start.40 = (f32[2,16,1]{2,1,0:T(8,128)S(1)}, f32[2,16,1]{2,1,0:T(8,128)S(1)}, u32[]{:S(2)}, u32[]{:S(2)}) collective-permute-start(f32[2,16,1]{2,1,0:T(8,128)S(1)} %get-tuple-element.216), channel_id=1, source_target_pairs={{0,4},{1,5},{2,6},{3,7},{4,8},{5,9},{6,10},{7,11},{8,12},{9,13},{1... | collective-permute-start | bytes 392 | tf_op jit(solution)/shard_map/ppermute | solution.py:31
  530.5 15.1 %collective-permute-start.84 = (f32[2,16,1]{2,1,0:T(8,128)S(1)}, f32[2,16,1]{2,1,0:T(8,128)S(1)}, u32[]{:S(2)}, u32[]{:S(2)}) collective-permute-start(f32[2,16,1]{2,1,0:T(8,128)S(1)} %get-tuple-element.198), channel_id=1, source_target_pairs={{0,4},{1,5},{2,6},{3,7},{4,8},{5,9},{6,10},{7,11},{8,12},{9,13},{1... | collective-permute-start | bytes 392 | tf_op jit(solution)/shard_map/ppermute | solution.py:31
  (159 other events, 3551.4 us)
